TPU v7x, 32 devices: a whole 2x2x4 slice. The times are simulated.
32 devices in a mesh: ctx: 8 (over z, x), ch: 4 (over y, core).
Axes of the slice: x: 2, y: 2, z: 4, core: 2. Of those that a mesh axis runs over, the one named last changes fastest.
Arguments:
- tokens: bfloat16 [1024, 4096], P('ctx'), may hold values from -6 to 6
- projections: bfloat16 [3, 4096, 4096], P(None, 'ctx', 'ch'), may hold values from -0.09375 to 0.09375
- decay_rates: float32 [4096, 16], P('ch'), may hold values from 0.00048828125 to 0.03
- residues: float32 [4096, 16], P('ch'), may hold values from -1.5 to 1.5
- short_filter: bfloat16 [4096, 128], P('ch'), may hold values from -0.5 to 0.5
Outputs:
- mixed: bfloat16 [1024, 4096], P('ctx', 'ch')
All inputs are finite; a program needn't handle non-finite values.
Results may differ from a plain program's by a relative error of at most 0.0068.
Values may be sent and summed in bfloat16 or wider, within the bound.
A program may use at most 64 MiB of HBM per device.

v0:
```python
import math

import jax
import jax.numpy as jnp
from jax import lax
from jax.sharding import PartitionSpec as P

two_pi = 2.0 * math.pi
highest = lax.Precision.HIGHEST


def angle_table(first_ids, second_ids, length):
    products = first_ids[:, None] * second_ids[None, :] % length
    angles = products.astype(jnp.float32) * (two_pi / length)
    return (jnp.cos(angles), jnp.sin(angles))


def twist(real_part, imag_part, cosine_table, sine_table, direction):
    return (
        real_part * cosine_table - direction * imag_part * sine_table,
        imag_part * cosine_table + direction * real_part * sine_table,
    )


def complex_apply(einsum_form, cosine_table, sine_table, real_part, imag_part, direction):
    cos_real = jnp.einsum(einsum_form, cosine_table, real_part, precision=highest)
    cos_imag = jnp.einsum(einsum_form, cosine_table, imag_part, precision=highest)
    sin_real = jnp.einsum(einsum_form, sine_table, real_part, precision=highest)
    sin_imag = jnp.einsum(einsum_form, sine_table, imag_part, precision=highest)
    return (cos_real - direction * sin_imag, cos_imag + direction * sin_real)


def filter_values(positions, rates_t, residues_t):
    terms = residues_t * jnp.sqrt(2.0 * rates_t) * jnp.exp(-rates_t * positions[None])
    return jnp.sum(terms, axis=0)


def toeplitz(taps_table):
    channels = taps_table.shape[0]
    tap_count = taps_table.shape[1]
    zero_block = jnp.zeros((channels, tap_count), taps_table.dtype)
    unrolled = jnp.concatenate([zero_block, jnp.flip(taps_table, axis=1), zero_block], axis=1)
    tiled = jnp.tile(unrolled, (1, tap_count))
    tiled = tiled[:, : tap_count * (3 * tap_count - 1)].reshape(
        channels, tap_count, 3 * tap_count - 1
    )
    return tiled[:, :, tap_count - 1 : 3 * tap_count - 1]


def project(tokens, projections):
    einsum_form = "td,kdc->kct"
    running = jnp.einsum(
        einsum_form,
        tokens,
        lax.all_gather(projections, "ctx", axis=1, tiled=True),
        preferred_element_type=jnp.float32,
    )
    return running.astype(jnp.bfloat16)


def per_device(tokens, projections, decay_rates, residues, short_filter):
    ctx_count = lax.axis_size("ctx")
    ctx_index = lax.axis_index("ctx")
    tok_rows = tokens.shape[0]
    channels = projections.shape[2]
    group_width = channels // ctx_count
    block_count = 2 * ctx_count
    full_length = tok_rows * block_count
    seq_length = tok_rows * ctx_count
    tap_count = short_filter.shape[1]
    block_ids = jnp.arange(block_count, dtype=jnp.int32)
    source_ids = jnp.arange(ctx_count, dtype=jnp.int32)
    row_ids = jnp.arange(tok_rows, dtype=jnp.int32)
    cos_block, sin_block = angle_table(block_ids, source_ids, block_count)
    cos_row, sin_row = angle_table(row_ids, row_ids, tok_rows)
    streams = project(tokens, projections)
    arrived_streams = lax.all_to_all(streams, "ctx", split_axis=1, concat_axis=2, tiled=True)
    signal = arrived_streams[0].astype(jnp.float32) * arrived_streams[1].astype(jnp.float32)
    own_rates = lax.dynamic_slice_in_dim(decay_rates, ctx_index * group_width, group_width, 0)
    own_residues = lax.dynamic_slice_in_dim(residues, ctx_index * group_width, group_width, 0)
    positions = jnp.arange(seq_length, dtype=jnp.float32)[None, :]
    impulse = filter_values(positions, own_rates.T[:, :, None], own_residues.T[:, :, None])
    cos_twist, sin_twist = angle_table(block_ids, row_ids, full_length)

    def to_spectrum(sequence_values):
        shaped = sequence_values.reshape(group_width, ctx_count, tok_rows)
        real_part = jnp.einsum("aq,cqr->car", cos_block, shaped, precision=highest)
        imag_part = -jnp.einsum("aq,cqr->car", sin_block, shaped, precision=highest)
        real_part, imag_part = twist(real_part, imag_part, cos_twist, sin_twist, -1.0)
        return complex_apply("br,car->cab", cos_row, sin_row, real_part, imag_part, -1.0)

    signal_real, signal_imag = to_spectrum(signal)
    impulse_real, impulse_imag = to_spectrum(impulse)
    product_real = signal_real * impulse_real - signal_imag * impulse_imag
    product_imag = signal_real * impulse_imag + signal_imag * impulse_real
    back_real, back_imag = complex_apply(
        "br,cab->car", cos_row, sin_row, product_real, product_imag, 1.0
    )
    back_real, back_imag = twist(back_real, back_imag, cos_twist, sin_twist, 1.0)
    convolved = (
        jnp.einsum("aq,car->cqr", cos_block, back_real, precision=highest)
        - jnp.einsum("aq,car->cqr", sin_block, back_imag, precision=highest)
    ) / full_length
    convolved = convolved.reshape(group_width, seq_length)
    gated_rows = (arrived_streams[2].astype(jnp.float32) * convolved).astype(jnp.bfloat16)
    own_taps = lax.dynamic_slice_in_dim(short_filter, ctx_index * group_width, group_width, 0)
    shaped = gated_rows.reshape(group_width, seq_length // tap_count, tap_count)
    previous = jnp.concatenate(
        [jnp.zeros((group_width, 1, tap_count), jnp.bfloat16), shaped[:, :-1]], axis=1
    )
    block_pairs = jnp.concatenate([previous, shaped], axis=2)
    filtered = jnp.einsum(
        "ckj,cbj->bkc", toeplitz(own_taps), block_pairs, preferred_element_type=jnp.float32
    )
    filtered = filtered.reshape(seq_length, group_width).astype(jnp.bfloat16)
    return lax.all_to_all(filtered, "ctx", split_axis=0, concat_axis=1, tiled=True)


def solution(mesh):
    in_specs = (P("ctx", None), P(None, "ctx", "ch"), P("ch", None), P("ch", None), P("ch", None))
    out_specs = P("ctx", "ch")
    return jax.shard_map(
        per_device, mesh=mesh, in_specs=in_specs, out_specs=out_specs, check_vma=False
    )
```

profile of v0, /device:TPU:0, one launch (start us, length us, event | category | flops | bytes accessed | tf_op | source)
XLA Modules:
  0.0 622.2 jit_solution(2238312228464869096)
XLA Ops:
  6.5 4.8 copy.70
  11.4 483.3 %all-gather.2.cloned.1.call-done = bf16[3,4096,1024]{1,2,0:T(8,128)(2,1)} async-done(((bf16[3,512,1024]{1,2,0:T(8,128)(2,1)}), bf16[3,4096,1024]{1,2,0:T(8,128)(2,1)}) %all-gather.2.cloned.1.call-update) | async-done | bytes 25165840 | tf_op jit(solution)/shard_map/all_gather | solution.py:55
  494.6 11.7 %convolution_convert_fusion = bf16[3,1024,128]{2,1,0:T(8,128)(2,1)S(1)} fusion(bf16[3,4096,1024]{1,2,0:T(8,128)(2,1)} %all-gather.2.cloned.1.call-done, bf16[128,4096]{1,0:T(8,128)(2,1)S(1)} %copy-done), kind=kOutput, calls=%fused_computation.3 | convolution fusion | flops 3221618688 | bytes 27000832 | tf_op jit(solution)/shard_map/td,kdc->kct/dot_general | solution.py:52
  506.3 1.7 copy.71
  508.1 4.6 all-to-all-start
  513.4 1.6 multiply_reduce_fusion
  516.0 5.6 tile.4
  521.6 12.5 %copy.97 = bf16[16,8,128,384]{3,1,2,0:T(8,128)(2,1)S(1)} copy(bf16[16,8,128,384]{3,2,1,0:T(8,128)(2,1)} %bitcast.92) | data formatting | bytes 25165824
  534.1 5.3 slice.31
  539.4 31.0 %reshape.74 = bf16[128,128,383]{2,1,0:T(8,128)(2,1)} reshape(bf16[128,49024]{1,0:T(8,128)(2,1)} %slice.31) | data formatting | bytes 25100288 | tf_op jit(solution)/shard_map/reshape | solution.py:44
  574.4 1.5 multiply_add_fusion.1
  576.0 1.4 fusion.33
  577.4 1.4 fusion.37
  578.9 1.4 fusion.4
  580.3 1.4 fusion.6
  581.8 1.7 fusion.43
  584.9 1.5 fusion.7
  586.4 1.7 multiply_subtract_fusion
  588.1 1.7 fusion.31
  589.8 1.7 fusion.27
  591.5 1.7 convolution_subtract_fusion
  593.3 1.7 convolution_add_fusion
  596.9 2.7 fusion.15
  599.7 14.4 %all_to_all.31 = bf16[8,128,128]{1,2,0:T(8,128)(2,1)S(1)} all-to-all(bf16[8,128,128]{1,2,0:T(8,128)(2,1)S(1)} %copy.86), channel_id=1, replica_groups=mesh['ctx'=8,'ch'=4] {'ctx'}, dimensions={0} | all-to-all | bytes 524288 | tf_op jit(solution)/shard_map/all_to_all | solution.py:116
  (31 shorter events, 10.0 us)
Async XLA Ops:
  6.5 488.1 %copy-start = (bf16[128,4096]{1,0:T(8,128)(2,1)S(1)}, bf16[128,4096]{1,0:T(8,128)(2,1)}, u32[]{:S(2)}) copy-start(bf16[128,4096]{1,0:T(8,128)(2,1)} %param.5) | copy-start | bytes 3145732
  6.5 488.1 %all-gather.2.cloned.1.call-start = ((), (), s32[]{:S(2)}) async-start(), calls=%async_computation.2 | async-start | bytes 28311552 | tf_op jit(solution)/shard_map/all_gather | solution.py:55
  508.1 63.5 %all-to-all-start = ((bf16[3,1024,128]{2,0,1:T(4,128)(2,1)}), bf16[3,1024,128]{2,0,1:T(4,128)(2,1)S(1)}, u32[]{:S(2)}, u32[]{:S(2)}) async-start(bf16[3,1024,128]{2,0,1:T(4,128)(2,1)} %copy.71), calls=%async_computation | async-start | bytes 2097152 | tf_op jit(solution)/shard_map/all_to_all | solution.py:77
  586.4 10.5 %slice-start = ((s8[12582912]{0:T(1024)(128)(4,1)}), s8[4194304]{0:T(1024)(128)(4,1)S(1)}, s32[]{:S(2)}) async-start(s8[12582912]{0:T(1024)(128)(4,1)} %bitcast.94), calls=%async_computation.3 | async-start | bytes 8388608
  588.0 8.9 %slice-start.1 = ((s8[12582912]{0:T(1024)(128)(4,1)}), s8[4194304]{0:T(1024)(128)(4,1)S(1)}, s32[]{:S(2)}) async-start(s8[12582912]{0:T(1024)(128)(4,1)} %bitcast.94), calls=%async_computation.4 | async-start | bytes 8388608
  593.2 3.7 slice-start.2
  593.2 21.7 %copy-start.1 = (bf16[128,4096]{1,0:T(8,128)(2,1)S(1)}, bf16[128,4096]{1,0:T(8,128)(2,1)}, u32[]{:S(2)}) copy-start(bf16[128,4096]{1,0:T(8,128)(2,1)} %param.5) | copy-start | bytes 3145732
Sparse Core Ops, SparseCore 0:
  11.5 483.1 all-gather.1
where the time goes:
time: 630 us; the launch traced here: 622 us
  waiting for transfers between devices  483 us (77%)
  local copies, waits for them, and re-layouts  63.4 us (10%)
  matrix products  39.9 us (6%)
  blocking collectives  14.4 us (2%)
  between operations  14.1 us (2%)
    all_gather x1, waiting for transfers between devices, project(): lax.all_gather(projections, 'ctx', axis=1, tiled=True)  483 us
    reshape x1, local copies, waits for them, and re-layouts, toeplitz(): tiled[:, :tap_count * (3 * tap_count - 1)]  31 us
    unnamed x13, local copies, waits for them, and re-layouts  17.4 us
    all_to_all x1, blocking collectives, per_device(): lax.all_to_all(filtered, 'ctx', split_axis=0, concat_axis=1, tiled=True)  14.4 us
  transfers between devices with their start and end apart: 2, of which 1 were waited for; matrix products, arithmetic and copies ran while one was open for 9% of the time, Pallas kernels for 0%

commit v1 on v0

--- a/solution.py
+++ b/solution.py
@@ -1,9 +1,414 @@
+import functools
 import math
 
 import jax
 import jax.numpy as jnp
 from jax import lax
+from jax.experimental import pallas as pl
+from jax.experimental.pallas import tpu as pltpu
 from jax.sharding import PartitionSpec as P
+
+MESH = pl.DeviceIdType.MESH
+PAIR = 2
+CHUNKS = 8
+LANES = 128
+
+
+def remote(src, dst, send_sem, recv_sem, device):
+    return pltpu.make_async_remote_copy(
+        src_ref=src, dst_ref=dst, send_sem=send_sem, recv_sem=recv_sem,
+        device_id=device, device_id_type=MESH,
+    )
+
+
+def project_kernel(
+    tok_ref, proj_ref, signal_ref, gate_ref,
+    tokb, wbuf, part, sendb, recvb,
+    local_sem, wl_sem, ws_sem, wr_sem,
+    tzs, tzr, txs, txr, tcs, tcr, ps_sem, pr_sem,
+):
+    rows = tok_ref.shape[0]
+    depth = proj_ref.shape[1]
+    width = wbuf.shape[3]
+    span = PAIR * depth
+    ctx_count = lax.axis_size("ctx")
+    zc = ctx_count // PAIR
+    seq = rows * ctx_count
+    ctx = lax.axis_index("ctx")
+    ch = lax.axis_index("ch")
+    mz, mx = ctx // PAIR, ctx % PAIR
+    core = ch % 2
+    mate = {"ch": ch + 1 - 2 * core}
+    across = {"ctx": ctx + 1 - 2 * mx}
+    half = rows // 2
+    low = (mz < zc // 2).astype(jnp.int32)
+
+    def at_z(z):
+        return {"ctx": z * PAIR + mx}
+
+    def order(i):
+        return low * (zc - 1 - i) + (1 - low) * i
+
+    def cols(z):
+        return pl.ds(pl.multiple_of(z * span, 128), span)
+
+    def block(z, x):
+        return pl.ds(pl.multiple_of((z * PAIR + x) * rows, 16), rows)
+
+    def half_block(z, x):
+        return pl.ds(pl.multiple_of((z * PAIR + x) * rows + core * half, 16), half)
+
+    def group(d, x):
+        return pl.ds(pl.multiple_of((d * PAIR + x) * width, 128), width)
+
+    k_rows = pl.ds(pl.multiple_of(mx * depth, 16), depth)
+    my_half = pl.ds(pl.multiple_of(core * half, 16), half)
+
+    own_tok = pltpu.make_async_copy(tok_ref.at[:, cols(mz)], tokb.at[block(mz, mx)], local_sem)
+    own_tok.start()
+    own_w = []
+    for i in range(zc):
+        d = order(i)
+        own_w.append(
+            pltpu.make_async_copy(
+                proj_ref.at[:, :, group(d, mx)], wbuf.at[d, :, k_rows], wl_sem.at[i]
+            )
+        )
+        own_w[-1].start()
+
+    barrier = pltpu.get_barrier_semaphore()
+    for o in range(1, zc):
+        pl.semaphore_signal(
+            barrier, inc=1, device_id=at_z((mz + o) % zc), device_id_type=MESH
+        )
+    pl.semaphore_signal(barrier, inc=1, device_id=across, device_id_type=MESH)
+    pl.semaphore_signal(barrier, inc=1, device_id=mate, device_id_type=MESH)
+    pl.semaphore_wait(barrier, zc + 1)
+
+    sent = []
+    z_copy, x_copy, c_copy, w_copy = {}, {}, {}, {}
+    for o in range(1, zc):
+        zt = (mz + o) % zc
+        z_copy[o] = remote(
+            tok_ref.at[my_half, cols(zt)], tokb.at[half_block(mz, mx)],
+            tzs.at[o], tzr.at[o], at_z(zt),
+        )
+        z_copy[o].start()
+    x_copy[0] = remote(
+        tok_ref.at[my_half, cols(mz)], tokb.at[half_block(mz, mx)],
+        txs.at[0], txr.at[0], across,
+    )
+    x_copy[0].start()
+
+    def send_weights(i):
+        d = order(i)
+        w_copy[i] = remote(
+            proj_ref.at[:, :, group(d, 1 - mx)], wbuf.at[d, :, k_rows],
+            ws_sem.at[i], wr_sem.at[i], across,
+        )
+        w_copy[i].start()
+
+    send_weights(0)
+    for o in range(1, zc):
+        zs = (mz + zc - o) % zc
+        z_copy[o].wait_recv()
+        here = tokb.at[half_block(zs, mx)]
+        x_copy[o] = remote(here, here, txs.at[o], txr.at[o], across)
+        x_copy[o].start()
+        c_copy[o] = remote(here, here, tcs.at[o], tcr.at[o], mate)
+        c_copy[o].start()
+    for i in range(1, zc):
+        send_weights(i)
+    for o in range(zc):
+        zs = (mz + zc - o) % zc
+        x_copy[o].wait_recv()
+        here = tokb.at[half_block(zs, 1 - mx)]
+        c_copy[zc + o] = remote(here, here, tcs.at[zc + o], tcr.at[zc + o], mate)
+        c_copy[zc + o].start()
+    for key in c_copy:
+        c_copy[key].wait_recv()
+    own_tok.wait()
+
+    tile = math.gcd(seq, 256)
+    interior = jnp.logical_and(mz > 0, mz < zc - 1)
+    at_end = jnp.logical_or(mz == 0, mz == zc - 1)
+
+    def hop(d):
+        right = (d > mz).astype(jnp.int32)
+        to = mz + 2 * right - 1
+        last = (d == to).astype(jnp.int32) * (1 - right)
+        slot = d + last * (zc - d)
+        return remote(sendb.at[d], recvb.at[slot], ps_sem.at[d], pr_sem.at[slot], at_z(to))
+
+    def incoming(slot):
+        return remote(sendb.at[0], recvb.at[slot], ps_sem.at[0], pr_sem.at[slot], at_z(mz))
+
+    def tile_rows(t):
+        return pl.ds(pl.multiple_of(t * tile, 16), tile)
+
+    for i in range(zc):
+        d = order(i)
+        own_w[i].wait()
+        w_copy[i].wait_recv()
+
+        @pl.loop(0, seq // tile)
+        def _(t):
+            here = tile_rows(t)
+            block_tok = tokb[here, :]
+            for k in range(3):
+                part[d, k, here, :] = jnp.dot(
+                    block_tok, wbuf[d, k], preferred_element_type=jnp.float32
+                )
+
+        @pl.when(jnp.logical_and(at_end, d != mz))
+        def _():
+            @pl.loop(0, seq // tile)
+            def _(t):
+                here = tile_rows(t)
+                for k in range(3):
+                    sendb[d, k, here, :] = part[d, k, here, :].astype(jnp.bfloat16)
+
+            hop(d).start()
+
+    def forward(d, wanted):
+        @pl.when(jnp.logical_and(interior, wanted))
+        def _():
+            incoming(d).wait_recv()
+
+            @pl.loop(0, seq // tile)
+            def _(t):
+                here = tile_rows(t)
+                for k in range(3):
+                    total = part[d, k, here, :] + recvb[d, k, here, :].astype(jnp.float32)
+                    sendb[d, k, here, :] = total.astype(jnp.bfloat16)
+
+            hop(d).start()
+
+    for j in range(zc - 1):
+        first = low * (zc - 1 - j) + (1 - low) * j
+        forward(first, (first - mz) * (2 * low - 1) > 0)
+        second = low * j + (1 - low) * (zc - 1 - j)
+        forward(second, (second - mz) * (2 * low - 1) < 0)
+
+    def absorb(slot):
+        incoming(slot).wait_recv()
+
+        @pl.loop(0, seq // tile)
+        def _(t):
+            here = tile_rows(t)
+            for k in range(3):
+                part[mz, k, here, :] += recvb[slot, k, here, :].astype(jnp.float32)
+
+    @pl.when(mz > 0)
+    def _():
+        absorb(mz)
+
+    @pl.when(mz < zc - 1)
+    def _():
+        absorb(zc)
+
+    @pl.loop(0, seq // tile)
+    def _(t):
+        here = tile_rows(t)
+        signal_ref[here, :] = part[mz, 0, here, :] * part[mz, 1, here, :]
+        gate_ref[here, :] = part[mz, 2, here, :]
+
+    for group_of in (z_copy, x_copy, c_copy, w_copy):
+        for key in group_of:
+            group_of[key].wait_send()
+    for d in range(zc):
+        @pl.when(d != mz)
+        def _():
+            hop(d).wait_send()
+
+
+def project(tokens, projections):
+    rows, features = tokens.shape
+    depth, channels = projections.shape[1:]
+    ctx_count = lax.axis_size("ctx")
+    zc = ctx_count // PAIR
+    width = channels // ctx_count
+    seq = rows * ctx_count
+    dma = pltpu.SemaphoreType.DMA
+    shape = jax.ShapeDtypeStruct((seq, width), jnp.float32)
+    return pl.pallas_call(
+        project_kernel,
+        out_shape=(shape, shape),
+        in_specs=[pl.BlockSpec(memory_space=pl.ANY)] * 2,
+        out_specs=(pl.BlockSpec(memory_space=pltpu.VMEM),) * 2,
+        scratch_shapes=[
+            pltpu.VMEM((seq, PAIR * depth), jnp.bfloat16),
+            pltpu.VMEM((zc, 3, PAIR * depth, width), jnp.bfloat16),
+            pltpu.VMEM((zc, 3, seq, width), jnp.float32),
+            pltpu.VMEM((zc, 3, seq, width), jnp.bfloat16),
+            pltpu.VMEM((zc + 1, 3, seq, width), jnp.bfloat16),
+            dma, dma((zc,)), dma((zc,)), dma((zc,)),
+            dma((zc,)), dma((zc,)), dma((zc,)), dma((zc,)),
+            dma((2 * zc,)), dma((2 * zc,)), dma((zc,)), dma((zc + 1,)),
+        ],
+        compiler_params=pltpu.CompilerParams(
+            collective_id=0, has_side_effects=True, vmem_limit_bytes=48 * 1024 * 1024
+        ),
+        name="project",
+    )(tokens, projections)
+
+
+def mix_kernel(
+    signal_ref, gate_ref, rates_ref, residues_ref, taps_ref, out_ref, gated, taps, mixed
+):
+    seq, width = signal_ref.shape
+    steps = seq // CHUNKS
+    modes = rates_ref.shape[1]
+    tap_count = taps_ref.shape[1]
+    own = pl.ds(pl.multiple_of(lax.axis_index("ctx") * width, 128), width)
+    rates = rates_ref[own, :].T
+    weights = residues_ref[own, :].T * jnp.sqrt(2.0 * rates)
+    taps[...] = taps_ref[own, :].astype(jnp.float32).T
+    wide = (CHUNKS, width)
+    decay = jnp.exp(-rates)
+    decays = [jnp.broadcast_to(decay[m : m + 1], wide) for m in range(modes)]
+    gains = [jnp.broadcast_to(weights[m : m + 1], wide) for m in range(modes)]
+    ids = lax.broadcasted_iota(jnp.int32, wide, 0)
+
+    def row(ref, s):
+        return ref[pl.ds(s, CHUNKS, stride=steps), :]
+
+    def advance(s, states):
+        x = row(signal_ref, s)
+        return tuple(decays[m] * states[m] + x for m in range(modes))
+
+    zero = jnp.zeros(wide, jnp.float32)
+    ends = lax.fori_loop(0, steps, advance, (zero,) * modes, unroll=4)
+    starts = []
+    for m in range(modes):
+        total = ends[m]
+        shift = 1
+        while shift < CHUNKS:
+            factor = jnp.exp(-rates[m : m + 1] * float(steps * shift))
+            total = total + jnp.where(ids >= shift, factor * pltpu.roll(total, shift, 0), 0.0)
+            shift *= 2
+        starts.append(jnp.where(ids >= 1, pltpu.roll(total, 1, 0), 0.0))
+
+    def emit(s, states):
+        states = advance(s, states)
+        terms = [gains[m] * states[m] for m in range(modes)]
+        while len(terms) > 1:
+            terms = [a + b for a, b in zip(terms[::2], terms[1::2])] + terms[len(terms) & ~1 :]
+        value = (row(gate_ref, s) * terms[0]).astype(jnp.bfloat16).astype(jnp.float32)
+        gated[steps + s] = value
+        gated[s] = jnp.where(ids >= 1, pltpu.roll(value, 1, 0), 0.0)
+        return states
+
+    lax.fori_loop(0, steps, emit, tuple(starts), unroll=2)
+
+    out_block, tap_block = 16, 8
+
+    @pl.loop(0, steps // out_block)
+    def _(b):
+        base = b * out_block
+
+        def add_taps(kb, sums):
+            first = steps + base - kb * tap_block - (tap_block - 1)
+            window = [gated[first + i] for i in range(out_block + tap_block - 1)]
+            sums = list(sums)
+            for k in range(tap_block):
+                tap = jnp.broadcast_to(taps[pl.ds(kb * tap_block + k, 1), :], wide)
+                for i in range(out_block):
+                    sums[i] = sums[i] + tap * window[i + tap_block - 1 - k]
+            return tuple(sums)
+
+        sums = lax.fori_loop(0, tap_count // tap_block, add_taps, (zero,) * out_block)
+        for i in range(out_block):
+            mixed[pl.ds(base + i, CHUNKS, stride=steps), :] = sums[i]
+
+    out_ref[...] = mixed[...].astype(out_ref.dtype)
+
+
+def mix(signal, gate, decay_rates, residues, short_filter):
+    seq, width = signal.shape
+    steps = seq // CHUNKS
+    tap_count = short_filter.shape[1]
+    return pl.pallas_call(
+        mix_kernel,
+        out_shape=jax.ShapeDtypeStruct((seq, width), jnp.bfloat16),
+        in_specs=[pl.BlockSpec(memory_space=pltpu.VMEM)] * 5,
+        out_specs=pl.BlockSpec(memory_space=pltpu.VMEM),
+        scratch_shapes=[
+            pltpu.VMEM((2 * steps, CHUNKS, width), jnp.float32),
+            pltpu.VMEM((tap_count, width), jnp.float32),
+            pltpu.VMEM((seq, width), jnp.float32),
+        ],
+        compiler_params=pltpu.CompilerParams(vmem_limit_bytes=32 * 1024 * 1024),
+        name="mix",
+    )(signal, gate, decay_rates, residues, short_filter)
+
+
+def spread_kernel(mixed_ref, out_ref, local_sem, send_sem, recv_sem):
+    ctx_count = lax.axis_size("ctx")
+    ctx = lax.axis_index("ctx")
+    rows = out_ref.shape[0]
+    width = mixed_ref.shape[1]
+    mine = pl.ds(pl.multiple_of(ctx * width, 128), width)
+
+    def rows_of(p):
+        return pl.ds(pl.multiple_of(p * rows, 16), rows)
+
+    own = pltpu.make_async_copy(mixed_ref.at[rows_of(ctx)], out_ref.at[:, mine], local_sem)
+    own.start()
+    barrier = pltpu.get_barrier_semaphore()
+    peers = [(ctx + o) % ctx_count for o in range(1, ctx_count)]
+    for p in peers:
+        pl.semaphore_signal(barrier, inc=1, device_id={"ctx": p}, device_id_type=MESH)
+    pl.semaphore_wait(barrier, ctx_count - 1)
+    copies = []
+    for o, p in enumerate(peers):
+        copies.append(
+            remote(
+                mixed_ref.at[rows_of(p)], out_ref.at[:, mine],
+                send_sem.at[o], recv_sem.at[o], {"ctx": p},
+            )
+        )
+        copies[-1].start()
+    own.wait()
+    for copy in copies:
+        copy.wait()
+
+
+def spread(mixed, channels):
+    seq, width = mixed.shape
+    ctx_count = lax.axis_size("ctx")
+    dma = pltpu.SemaphoreType.DMA
+    return pl.pallas_call(
+        spread_kernel,
+        out_shape=jax.ShapeDtypeStruct((seq // ctx_count, channels), mixed.dtype),
+        in_specs=[pl.BlockSpec(memory_space=pltpu.VMEM)],
+        out_specs=pl.BlockSpec(memory_space=pltpu.VMEM),
+        scratch_shapes=[dma, dma((ctx_count - 1,)), dma((ctx_count - 1,))],
+        compiler_params=pltpu.CompilerParams(collective_id=1, has_side_effects=True),
+        name="spread",
+    )(mixed)
+
+
+def per_device_kernels(tokens, projections, decay_rates, residues, short_filter):
+    signal, gate = project(tokens, projections)
+    mixed = mix(signal, gate, decay_rates, residues, short_filter)
+    return spread(mixed, projections.shape[2])
+
+
+def kernels_fit(tokens, projections, short_filter):
+    ctx_count = lax.axis_size("ctx")
+    ch_count = lax.axis_size("ch")
+    rows = tokens.shape[0]
+    depth, channels = projections.shape[1:]
+    steps = rows * ctx_count // CHUNKS
+    tap_count = short_filter.shape[1]
+    return (
+        ctx_count % PAIR == 0 and ctx_count > PAIR and ch_count % 2 == 0
+        and channels == ctx_count * LANES and rows % 32 == 0 and depth % 128 == 0
+        and steps % 16 == 0 and tap_count % 8 == 0 and tap_count <= steps
+        and rows * ctx_count <= 2048
+    )
+
 
 two_pi = 2.0 * math.pi
 highest = lax.Precision.HIGHEST
@@ -47,7 +452,7 @@
     return tiled[:, :, tap_count - 1 : 3 * tap_count - 1]
 
 
-def project(tokens, projections):
+def project_general(tokens, projections):
     einsum_form = "td,kdc->kct"
     running = jnp.einsum(
         einsum_form,
@@ -58,7 +463,7 @@
     return running.astype(jnp.bfloat16)
 
 
-def per_device(tokens, projections, decay_rates, residues, short_filter):
+def per_device_general(tokens, projections, decay_rates, residues, short_filter):
     ctx_count = lax.axis_size("ctx")
     ctx_index = lax.axis_index("ctx")
     tok_rows = tokens.shape[0]
@@ -73,7 +478,7 @@
     row_ids = jnp.arange(tok_rows, dtype=jnp.int32)
     cos_block, sin_block = angle_table(block_ids, source_ids, block_count)
     cos_row, sin_row = angle_table(row_ids, row_ids, tok_rows)
-    streams = project(tokens, projections)
+    streams = project_general(tokens, projections)
     arrived_streams = lax.all_to_all(streams, "ctx", split_axis=1, concat_axis=2, tiled=True)
     signal = arrived_streams[0].astype(jnp.float32) * arrived_streams[1].astype(jnp.float32)
     own_rates = lax.dynamic_slice_in_dim(decay_rates, ctx_index * group_width, group_width, 0)
@@ -116,6 +521,11 @@
     return lax.all_to_all(filtered, "ctx", split_axis=0, concat_axis=1, tiled=True)
 
 
+def per_device(tokens, projections, decay_rates, residues, short_filter):
+    plan = per_device_kernels if kernels_fit(tokens, projections, short_filter) else per_device_general
+    return plan(tokens, projections, decay_rates, residues, short_filter)
+
+
 def solution(mesh):
     in_specs = (P("ctx", None), P(None, "ctx", "ch"), P("ch", None), P("ch", None), P("ch", None))
     out_specs = P("ctx", "ch")

time: 630 us -> 115 us (0.18); the launches traced: 622 us -> 115 us
  waiting for transfers between devices: 483 us -> 0 us
  Pallas kernels: 0 us -> 107 us
  local copies, waits for them, and re-layouts: 63.4 us -> 7.6 us
  matrix products: 39.9 us -> 0 us
  blocking collectives: 14.4 us -> 0 us
  between operations: 14.1 us -> 0.07 us
    all_gather x1 -> x0, waiting for transfers between devices: 483 us -> none  [project(): lax.all_gather(projections, 'ctx', axis=1, tiled=True)]
    pallas_call x0 -> x3, Pallas kernels: none -> 107 us  [the longest x1 89.1 us: project(): pl.pallas_call(project_kernel, out_shape=(shape, shape), in_specs=[pl.Blo...]
    dot_general x20 -> x0, matrix products: 39.9 us -> none  [the longest x1 11.7 us: project(): jnp.einsum(einsum_form, tokens, lax.all_gather(projections, 'ctx', axis=1...]
    reshape x1 -> x0, local copies, waits for them, and re-layouts: 31 us -> none  [toeplitz(): tiled[:, :tap_count * (3 * tap_count - 1)]]
    all_to_all x1 -> x0, blocking collectives: 14.4 us -> none  [per_device(): lax.all_to_all(filtered, 'ctx', split_axis=0, concat_axis=1, tiled=True)]
    unnamed x13 -> x11, local copies, waits for them, and re-layouts: 17.4 us -> 7.6 us
  transfers between devices with their start and end apart: 2 -> 0, of which waited for: 1 -> 0; matrix products, arithmetic and copies ran while one was open for 9% -> 0% of each run, Pallas kernels for 0% -> 0%
where the time goes in v1:
time: 115 us
  Pallas kernels  107 us (93%)
  local copies, waits for them, and re-layouts  7.6 us (7%)
    pallas_call x1, Pallas kernels, project(): pl.pallas_call(project_kernel, out_shape=(shape, shape), in_specs=[pl.Blo...  89.1 us
    pallas_call x1, Pallas kernels, spread(): pl.pallas_call(spread_kernel, out_shape=jax.ShapeDtypeStruct((seq // ctx_...  9.2 us
    pallas_call x1, Pallas kernels, mix(): pl.pallas_call(mix_kernel, out_shape=jax.ShapeDtypeStruct((seq, width), j...  9.13 us
    unnamed x11, local copies, waits for them, and re-layouts  7.6 us

profile of v1, /device:TPU:0, one launch (start us, length us, event | category | flops | bytes accessed | tf_op | source)
XLA Modules:
  0.0 115.1 jit_solution(3887830614427396196)
XLA Ops:
  0.0 0.0 copy-start.3
  0.0 1.1 copy.6.rates_ref
  1.1 1.0 copy.7.residues_ref
  2.1 0.0 copy-start
  2.1 1.9 %copy-done = bf16[3,512,1024]{2,1,0:T(8,128)(2,1)S(1)} copy-done((bf16[3,512,1024]{2,1,0:T(8,128)(2,1)S(1)}, bf16[3,512,1024]{2,1,0:T(8,128)(2,1)}, u32[]{:S(2)}) %copy-start) | copy-done | bytes 3145752
  4.0 0.0 copy-start.2
  4.0 1.2 %copy-done.2 = bf16[128,4096]{1,0:T(8,128)(2,1)S(1)} copy-done((bf16[128,4096]{1,0:T(8,128)(2,1)S(1)}, bf16[128,4096]{1,0:T(8,128)(2,1)}, u32[]{:S(2)}) %copy-start.2) | copy-done | bytes 1048600
  5.3 89.1 %project.1 = (f32[1024,128]{1,0:T(8,128)S(1)}, f32[1024,128]{1,0:T(8,128)S(1)}) custom-call(bf16[128,4096]{1,0:T(8,128)(2,1)S(1)} %copy-done.2, bf16[3,512,1024]{2,1,0:T(8,128)(2,1)S(1)} %copy-done), custom_call_target="tpu_custom_call" | custom-call | tf_op jit(solution)/shard_map/project/pallas_call | solution.py:234
  94.3 0.0 copy-done.3
  94.3 9.1 %mix.1.mixed_ref = bf16[1024,128]{1,0:T(8,128)(2,1)S(1)} custom-call(f32[1024,128]{1,0:T(8,128)S(1)} %get-tuple-element.7.signal_ref, f32[1024,128]{1,0:T(8,128)S(1)} %get-tuple-element.8.gate_ref, f32[1024,16]{1,0:T(8,128)S(1)} %copy.6.rates_ref, f32[1024,16]{1,0:T(8,128)S(1)} %copy.7.residues_ref, bf16[1024,128]{1,0:T(8,128)(2,1)S(1)} %copy-done.3), custom_call_target="tpu_custom_call" | custom-call | tf_op jit(solution)/shard_map/mix/pallas_call | solution.py:331
  103.5 0.0 copy-start.1
  103.5 0.7 copy-done.1
  104.2 9.2 %spread.1 = bf16[128,1024]{1,0:T(8,128)(2,1)} custom-call(bf16[1024,128]{1,0:T(8,128)(2,1)} %copy-done.1), custom_call_target="tpu_custom_call" | custom-call | tf_op jit(solution)/shard_map/spread/pallas_call | solution.py:381
  113.4 1.7 %copy.9 = bf16[128,1024]{1,0:T(8,128)(2,1)} copy(bf16[128,1024]{1,0:T(8,128)(2,1)} %spread.1) | data formatting | bytes 524288
Async XLA Ops:
  0.0 94.3 %copy-start.3 = (bf16[1024,128]{1,0:T(8,128)(2,1)S(1)}, bf16[1024,128]{1,0:T(8,128)(2,1)}, u32[]{:S(2)}) copy-start(bf16[1024,128]{1,0:T(8,128)(2,1)} %taps_ref.1) | copy-start | bytes 786436
  2.1 1.9 %copy-start = (bf16[3,512,1024]{2,1,0:T(8,128)(2,1)S(1)}, bf16[3,512,1024]{2,1,0:T(8,128)(2,1)}, u32[]{:S(2)}) copy-start(bf16[3,512,1024]{2,1,0:T(8,128)(2,1)} %proj_ref.1) | copy-start | bytes 9437188
  4.0 1.2 %copy-start.2 = (bf16[128,4096]{1,0:T(8,128)(2,1)S(1)}, bf16[128,4096]{1,0:T(8,128)(2,1)}, u32[]{:S(2)}) copy-start(bf16[128,4096]{1,0:T(8,128)(2,1)} %tok_ref.1) | copy-start | bytes 3145732
  103.5 0.7 copy-start.1

commit v2 on v0

--- a/solution.py
+++ b/solution.py
@@ -3,7 +3,17 @@
 import jax
 import jax.numpy as jnp
 from jax import lax
+from jax.experimental import pallas as pl
+from jax.experimental.pallas import tpu as pltpu
 from jax.sharding import PartitionSpec as P
+
+MESH = pl.DeviceIdType.MESH
+PAIR = 2
+CHUNKS = 8
+LANES = 128
+TILE = 256
+PIECES = 2
+
 
 two_pi = 2.0 * math.pi
 highest = lax.Precision.HIGHEST
@@ -47,7 +57,7 @@
     return tiled[:, :, tap_count - 1 : 3 * tap_count - 1]
 
 
-def project(tokens, projections):
+def project_general(tokens, projections):
     einsum_form = "td,kdc->kct"
     running = jnp.einsum(
         einsum_form,
@@ -58,7 +68,7 @@
     return running.astype(jnp.bfloat16)
 
 
-def per_device(tokens, projections, decay_rates, residues, short_filter):
+def per_device_general(tokens, projections, decay_rates, residues, short_filter):
     ctx_count = lax.axis_size("ctx")
     ctx_index = lax.axis_index("ctx")
     tok_rows = tokens.shape[0]
@@ -73,7 +83,7 @@
     row_ids = jnp.arange(tok_rows, dtype=jnp.int32)
     cos_block, sin_block = angle_table(block_ids, source_ids, block_count)
     cos_row, sin_row = angle_table(row_ids, row_ids, tok_rows)
-    streams = project(tokens, projections)
+    streams = project_general(tokens, projections)
     arrived_streams = lax.all_to_all(streams, "ctx", split_axis=1, concat_axis=2, tiled=True)
     signal = arrived_streams[0].astype(jnp.float32) * arrived_streams[1].astype(jnp.float32)
     own_rates = lax.dynamic_slice_in_dim(decay_rates, ctx_index * group_width, group_width, 0)
@@ -116,6 +126,410 @@
     return lax.all_to_all(filtered, "ctx", split_axis=0, concat_axis=1, tiled=True)
 
 
+def remote(src, dst, send_sem, recv_sem, device):
+    return pltpu.make_async_remote_copy(
+        src_ref=src, dst_ref=dst, send_sem=send_sem, recv_sem=recv_sem,
+        device_id=device, device_id_type=MESH,
+    )
+
+
+def block_kernel(
+    tok_ref, proj_ref, rates_ref, residues_ref, filter_ref, out_ref,
+    tokb, wbuf, sendb, recvb, ratesb, residuesb, filterb,
+    signal, gate, gated, taps, mixed, outb,
+    local_sem, par_sem, wl_sem, ws_sem, wr_sem,
+    tzs, tzr, txs, txr, tcs, tcr, ps_sem, pr_sem, ol_sem, os_sem, or_sem,
+):
+    rows = tok_ref.shape[0]
+    depth = proj_ref.shape[1]
+    width = wbuf.shape[3]
+    span = PAIR * depth
+    ctx_count = lax.axis_size("ctx")
+    zc = ctx_count // PAIR
+    held = zc // 2
+    seq = rows * ctx_count
+    steps = seq // CHUNKS
+    tile = sendb.shape[2] // pr_sem.shape[1]
+    tiles = seq // tile
+    modes = rates_ref.shape[0]
+    tap_count = filter_ref.shape[1]
+    ctx = lax.axis_index("ctx")
+    ch = lax.axis_index("ch")
+    mz, mx = ctx // PAIR, ctx % PAIR
+    core = ch % 2
+    mate = {"ch": ch + 1 - 2 * core}
+    across = {"ctx": ctx + 1 - 2 * mx}
+    half = rows // 2
+    low = (mz < held).astype(jnp.int32)
+    at_end = jnp.logical_or(mz == 0, mz == zc - 1)
+    interior = jnp.logical_and(mz > 0, mz < zc - 1)
+
+    def at_z(z):
+        return {"ctx": z * PAIR + mx}
+
+    def near(j):
+        return low * (zc - 1 - j) + (1 - low) * j
+
+    def far(j):
+        return low * j + (1 - low) * (zc - 1 - j)
+
+    def order(i):
+        return near(i // 2) if i % 2 == 0 else far(i // 2)
+
+    def cols(z):
+        return pl.ds(pl.multiple_of(z * span, 128), span)
+
+    def block(z, x):
+        return pl.ds(pl.multiple_of((z * PAIR + x) * rows, 16), rows)
+
+    def half_block(z, x):
+        return pl.ds(pl.multiple_of((z * PAIR + x) * rows + core * half, 16), half)
+
+    def group(d, x):
+        return pl.ds(pl.multiple_of((d * PAIR + x) * width, 128), width)
+
+    def tile_rows(t):
+        return pl.ds(pl.multiple_of(t * tile, 16), tile)
+
+    k_rows = pl.ds(pl.multiple_of(mx * depth, 16), depth)
+    my_half = pl.ds(pl.multiple_of(core * half, 16), half)
+
+    own_tok = pltpu.make_async_copy(tok_ref.at[:, cols(mz)], tokb.at[block(mz, mx)], local_sem)
+    own_tok.start()
+    own_w = []
+    for i in range(zc):
+        d = order(i)
+        own_w.append(
+            pltpu.make_async_copy(
+                proj_ref.at[:, :, group(d, mx)], wbuf.at[d, :, k_rows], wl_sem.at[i]
+            )
+        )
+        own_w[-1].start()
+    own_par = []
+    for j in range(held):
+        place = group(far(j), mx)
+        for n, (from_ref, to_ref) in enumerate((
+            (rates_ref.at[:, place], ratesb.at[j]),
+            (residues_ref.at[:, place], residuesb.at[j]),
+            (filter_ref.at[place, :], filterb.at[j]),
+        )):
+            own_par.append(pltpu.make_async_copy(from_ref, to_ref, par_sem.at[3 * j + n]))
+            own_par[-1].start()
+
+    barrier = pltpu.get_barrier_semaphore()
+    for o in range(1, ctx_count):
+        pl.semaphore_signal(
+            barrier, inc=1, device_id={"ctx": (ctx + o) % ctx_count}, device_id_type=MESH
+        )
+    pl.semaphore_signal(barrier, inc=1, device_id=mate, device_id_type=MESH)
+    pl.semaphore_wait(barrier, ctx_count)
+
+    z_copy, x_copy, c_copy, w_copy = {}, {}, {}, {}
+    for o in range(1, zc):
+        zt = (mz + o) % zc
+        z_copy[o] = remote(
+            tok_ref.at[my_half, cols(zt)], tokb.at[half_block(mz, mx)],
+            tzs.at[o], tzr.at[o], at_z(zt),
+        )
+        z_copy[o].start()
+    x_copy[0] = remote(
+        tok_ref.at[my_half, cols(mz)], tokb.at[half_block(mz, mx)],
+        txs.at[0], txr.at[0], across,
+    )
+    x_copy[0].start()
+
+    def send_weights(i):
+        d = order(i)
+        w_copy[i] = remote(
+            proj_ref.at[:, :, group(d, 1 - mx)], wbuf.at[d, :, k_rows],
+            ws_sem.at[i], wr_sem.at[i], across,
+        )
+        w_copy[i].start()
+
+    send_weights(0)
+    for o in range(1, zc):
+        zs = (mz + zc - o) % zc
+        z_copy[o].wait_recv()
+        here = tokb.at[half_block(zs, mx)]
+        x_copy[o] = remote(here, here, txs.at[o], txr.at[o], across)
+        x_copy[o].start()
+        c_copy[o] = remote(here, here, tcs.at[o], tcr.at[o], mate)
+        c_copy[o].start()
+    for i in range(1, zc):
+        send_weights(i)
+    for o in range(zc):
+        zs = (mz + zc - o) % zc
+        x_copy[o].wait_recv()
+        here = tokb.at[half_block(zs, 1 - mx)]
+        c_copy[zc + o] = remote(here, here, tcs.at[zc + o], tcr.at[zc + o], mate)
+        c_copy[zc + o].start()
+    for key in c_copy:
+        c_copy[key].wait_recv()
+    own_tok.wait()
+
+    def hop(d, t):
+        to = mz + 2 * (d >= held).astype(jnp.int32) - 1
+        here = tile_rows(t)
+        return remote(
+            sendb.at[d, :, here, :], recvb.at[d, :, here, :],
+            ps_sem.at[d, t], pr_sem.at[d, t], at_z(to),
+        )
+
+    def weights_here(i):
+        own_w[i].wait()
+        w_copy[i].wait_recv()
+
+    def products(d, t):
+        block_tok = tokb[tile_rows(t), :]
+        return [
+            jnp.dot(block_tok, wbuf[d, k], preferred_element_type=jnp.float32)
+            for k in range(3)
+        ]
+
+    def arrived(d, t):
+        here = tile_rows(t)
+        pltpu.make_async_copy(
+            sendb.at[d, :, here, :], recvb.at[d, :, here, :], pr_sem.at[d, t]
+        ).wait()
+        return [recvb[d, k, here, :].astype(jnp.float32) for k in range(3)]
+
+    def pass_on(d, t):
+        mine = products(d, t)
+        before = arrived(d, t)
+        for k in range(3):
+            sendb[d, k, tile_rows(t), :] = (mine[k] + before[k]).astype(jnp.bfloat16)
+        hop(d, t).start()
+
+    @pl.when(interior)
+    def _():
+        for j in range(held):
+            weights_here(2 * j)
+            weights_here(2 * j + 1)
+
+            @pl.loop(0, tiles)
+            def _(t):
+                pass_on(near(j), t)
+
+                @pl.when(t > 0)
+                def _():
+                    pass_on(far(j), t - 1)
+
+            pass_on(far(j), tiles - 1)
+
+    wide = (CHUNKS, width)
+    zero = jnp.zeros(wide, jnp.float32)
+    peers = [(ctx + o) % ctx_count for o in range(1, ctx_count)]
+    piece = rows // PIECES
+
+    def leave(j, h, o):
+        p = peers[o]
+        here = pl.ds(pl.multiple_of(p * rows + h * piece, 16), piece)
+        place = far(j) * PAIR + mx
+        return remote(
+            outb.at[j, here, :], out_ref.at[pl.ds(h * piece, piece), group(far(j), mx)],
+            os_sem.at[j, h, o], or_sem.at[place, h], {"ctx": p},
+        )
+
+    def stay(j):
+        here = pl.ds(pl.multiple_of(ctx * rows, 16), rows)
+        return pltpu.make_async_copy(
+            outb.at[j, here, :], out_ref.at[:, group(far(j), mx)], ol_sem.at[j]
+        )
+
+    def mix(j):
+        rates = ratesb[j]
+        weights = residuesb[j] * jnp.sqrt(2.0 * rates)
+        taps[...] = filterb[j].astype(jnp.float32).T
+        decay = jnp.exp(-rates)
+        decays = [jnp.broadcast_to(decay[m : m + 1], wide) for m in range(modes)]
+        gains = [jnp.broadcast_to(weights[m : m + 1], wide) for m in range(modes)]
+        ids = lax.broadcasted_iota(jnp.int32, wide, 0)
+
+        def row(ref, s):
+            return ref[pl.ds(s, CHUNKS, stride=steps), :]
+
+        def advance(s, states):
+            x = row(signal, s)
+            return tuple(decays[m] * states[m] + x for m in range(modes))
+
+        ends = lax.fori_loop(0, steps, advance, (zero,) * modes, unroll=4)
+        starts = []
+        for m in range(modes):
+            total = ends[m]
+            shift = 1
+            while shift < CHUNKS:
+                factor = jnp.exp(-rates[m : m + 1] * float(steps * shift))
+                total = total + jnp.where(ids >= shift, factor * pltpu.roll(total, shift, 0), 0.0)
+                shift *= 2
+            starts.append(jnp.where(ids >= 1, pltpu.roll(total, 1, 0), 0.0))
+
+        def emit(s, states):
+            states = advance(s, states)
+            terms = [gains[m] * states[m] for m in range(modes)]
+            while len(terms) > 1:
+                terms = [a + b for a, b in zip(terms[::2], terms[1::2])] + terms[len(terms) & ~1 :]
+            value = row(gate, s) * terms[0]
+            gated[steps + s] = value
+            gated[s] = jnp.where(ids >= 1, pltpu.roll(value, 1, 0), 0.0)
+            return states
+
+        lax.fori_loop(0, steps, emit, tuple(starts), unroll=2)
+
+        out_block, tap_block = 16, 8
+        for h in range(PIECES):
+            @pl.loop(h * piece // out_block, (h + 1) * piece // out_block)
+            def _(b):
+                base = b * out_block
+
+                def add_taps(kb, sums):
+                    first = steps + base - kb * tap_block - (tap_block - 1)
+                    window = [gated[first + i] for i in range(out_block + tap_block - 1)]
+                    sums = list(sums)
+                    for k in range(tap_block):
+                        tap = jnp.broadcast_to(taps[pl.ds(kb * tap_block + k, 1), :], wide)
+                        for i in range(out_block):
+                            sums[i] = sums[i] + tap * window[i + tap_block - 1 - k]
+                    return tuple(sums)
+
+                sums = lax.fori_loop(0, tap_count // tap_block, add_taps, (zero,) * out_block)
+                for i in range(out_block):
+                    mixed[pl.ds(base + i, CHUNKS, stride=steps), :] = sums[i]
+
+            for c in range(CHUNKS):
+                here = pl.ds(c * rows + h * piece, piece)
+                outb[j, here, :] = mixed[here, :].astype(outb.dtype)
+            for o in range(ctx_count - 1):
+                leave(j, h, o).start()
+        stay(j).start()
+
+    @pl.when(at_end)
+    def _():
+        for j in range(held):
+            weights_here(2 * j)
+
+            @pl.loop(0, tiles)
+            def _(t):
+                mine = products(near(j), t)
+                for k in range(3):
+                    sendb[near(j), k, tile_rows(t), :] = mine[k].astype(jnp.bfloat16)
+                hop(near(j), t).start()
+
+        for j in range(held):
+            weights_here(2 * j + 1)
+            for n in range(3):
+                own_par[3 * j + n].wait()
+
+            @pl.loop(0, tiles)
+            def _(t):
+                mine = products(far(j), t)
+                before = arrived(far(j), t)
+                sums = [mine[k] + before[k] for k in range(3)]
+                signal[tile_rows(t), :] = sums[0] * sums[1]
+                gate[tile_rows(t), :] = sums[2]
+
+            mix(j)
+
+        for j in range(held):
+            stay(j).wait()
+
+            @pl.loop(0, tiles)
+            def _(t):
+                hop(near(j), t).wait_send()
+
+            for h in range(PIECES):
+                for o in range(ctx_count - 1):
+                    leave(j, h, o).wait_send()
+
+    @pl.when(interior)
+    def _():
+        for par in own_par:
+            par.wait()
+        for j in range(held):
+            @pl.loop(0, tiles)
+            def _(t):
+                hop(near(j), t).wait_send()
+                hop(far(j), t).wait_send()
+
+    for group_of in (z_copy, x_copy, c_copy, w_copy):
+        for key in group_of:
+            group_of[key].wait_send()
+    for d in range(zc):
+        owner_row = 0 if d < held else zc - 1
+        for x in range(PAIR):
+            @pl.when(ctx != owner_row * PAIR + x)
+            def _():
+                for h in range(PIECES):
+                    landed = out_ref.at[
+                        pl.ds(h * piece, piece), pl.ds((d * PAIR + x) * width, width)
+                    ]
+                    pltpu.make_async_copy(
+                        outb.at[0, pl.ds(0, piece), :], landed, or_sem.at[d * PAIR + x, h]
+                    ).wait()
+
+
+def per_device_kernels(tokens, projections, decay_rates, residues, short_filter):
+    rows = tokens.shape[0]
+    depth, channels = projections.shape[1:]
+    ctx_count = lax.axis_size("ctx")
+    zc = ctx_count // PAIR
+    held = zc // 2
+    width = channels // ctx_count
+    seq = rows * ctx_count
+    steps = seq // CHUNKS
+    tiles = seq // TILE
+    modes = decay_rates.shape[1]
+    tap_count = short_filter.shape[1]
+    dma = pltpu.SemaphoreType.DMA
+    f32, bf16 = jnp.float32, jnp.bfloat16
+    return pl.pallas_call(
+        block_kernel,
+        out_shape=jax.ShapeDtypeStruct((rows, channels), bf16),
+        in_specs=[pl.BlockSpec(memory_space=pl.ANY)] * 5,
+        out_specs=pl.BlockSpec(memory_space=pltpu.VMEM),
+        scratch_shapes=[
+            pltpu.VMEM((seq, PAIR * depth), bf16),
+            pltpu.VMEM((zc, 3, PAIR * depth, width), bf16),
+            pltpu.VMEM((zc, 3, seq, width), bf16),
+            pltpu.VMEM((zc, 3, seq, width), bf16),
+            pltpu.VMEM((held, modes, width), f32),
+            pltpu.VMEM((held, modes, width), f32),
+            pltpu.VMEM((held, width, tap_count), bf16),
+            pltpu.VMEM((seq, width), f32),
+            pltpu.VMEM((seq, width), f32),
+            pltpu.VMEM((2 * steps, CHUNKS, width), f32),
+            pltpu.VMEM((tap_count, width), f32),
+            pltpu.VMEM((seq, width), f32),
+            pltpu.VMEM((held, seq, width), bf16),
+            dma, dma((3 * held,)), dma((zc,)), dma((zc,)), dma((zc,)),
+            dma((zc,)), dma((zc,)), dma((zc,)), dma((zc,)),
+            dma((2 * zc,)), dma((2 * zc,)), dma((zc, tiles)), dma((zc, tiles)),
+            dma((held,)), dma((held, PIECES, ctx_count - 1)), dma((ctx_count, PIECES)),
+        ],
+        compiler_params=pltpu.CompilerParams(
+            collective_id=0, has_side_effects=True, vmem_limit_bytes=48 * 1024 * 1024
+        ),
+        name="block",
+    )(tokens, projections, decay_rates.T, residues.T, short_filter)
+
+
+def kernels_fit(tokens, projections, short_filter):
+    ctx_count = lax.axis_size("ctx")
+    rows = tokens.shape[0]
+    depth, channels = projections.shape[1:]
+    tap_count = short_filter.shape[1]
+    return (
+        ctx_count == CHUNKS and lax.axis_size("ch") % 2 == 0
+        and channels == ctx_count * LANES and rows % (16 * PIECES) == 0 and depth % 128 == 0
+        and (rows * ctx_count) % TILE == 0 and tap_count % 8 == 0 and tap_count <= rows
+        and rows * ctx_count <= 2048
+    )
+
+
+def per_device(tokens, projections, decay_rates, residues, short_filter):
+    plan = per_device_kernels if kernels_fit(tokens, projections, short_filter) else per_device_general
+    return plan(tokens, projections, decay_rates, residues, short_filter)
+
+
 def solution(mesh):
     in_specs = (P("ctx", None), P(None, "ctx", "ch"), P("ch", None), P("ch", None), P("ch", None))
     out_specs = P("ctx", "ch")

time: 630 us -> 106 us (0.17); the launches traced: 622 us -> 105 us
  waiting for transfers between devices: 483 us -> 0 us
  Pallas kernels: 0 us -> 98.9 us
  local copies, waits for them, and re-layouts: 63.4 us -> 6.45 us
  matrix products: 39.9 us -> 0 us
  blocking collectives: 14.4 us -> 0 us
  between operations: 14.1 us -> 0.01 us
    all_gather x1 -> x0, waiting for transfers between devices: 483 us -> none  [project(): lax.all_gather(projections, 'ctx', axis=1, tiled=True)]
    pallas_call x0 -> x1, Pallas kernels: none -> 98.9 us  [per_device_kernels(): pl.pallas_call(block_kernel, out_shape=jax.ShapeDtypeStruct((rows, channe...]
    dot_general x20 -> x0, matrix products: 39.9 us -> none  [the longest x1 11.7 us: project(): jnp.einsum(einsum_form, tokens, lax.all_gather(projections, 'ctx', axis=1...]
    reshape x1 -> x0, local copies, waits for them, and re-layouts: 31 us -> none  [toeplitz(): tiled[:, :tap_count * (3 * tap_count - 1)]]
    all_to_all x1 -> x0, blocking collectives: 14.4 us -> none  [per_device(): lax.all_to_all(filtered, 'ctx', split_axis=0, concat_axis=1, tiled=True)]
    unnamed x13 -> x11, local copies, waits for them, and re-layouts: 17.4 us -> 6.45 us
  transfers between devices with their start and end apart: 2 -> 0, of which waited for: 1 -> 0; matrix products, arithmetic and copies ran while one was open for 9% -> 0% of each run, Pallas kernels for 0% -> 0%
where the time goes in v2:
time: 106 us; the launch traced here: 105 us
  Pallas kernels  98.9 us (93%)
  local copies, waits for them, and re-layouts  6.45 us (6%)
    pallas_call x1, Pallas kernels, per_device_kernels(): pl.pallas_call(block_kernel, out_shape=jax.ShapeDtypeStruct((rows, channe...  98.9 us
    unnamed x11, local copies, waits for them, and re-layouts  6.45 us

profile of v2, /device:TPU:0, one launch (start us, length us, event | category | flops | bytes accessed | tf_op | source)
XLA Modules:
  0.0 105.4 jit_solution(14312386471391102149)
XLA Ops:
  0.0 0.0 copy-start
  0.0 1.9 %copy-done = bf16[3,512,1024]{2,1,0:T(8,128)(2,1)S(1)} copy-done((bf16[3,512,1024]{2,1,0:T(8,128)(2,1)S(1)}, bf16[3,512,1024]{2,1,0:T(8,128)(2,1)}, u32[]{:S(2)}) %copy-start) | copy-done | bytes 3145752
  1.9 0.0 copy-start.1
  1.9 1.2 %copy-done.1 = bf16[128,4096]{1,0:T(8,128)(2,1)S(1)} copy-done((bf16[128,4096]{1,0:T(8,128)(2,1)S(1)}, bf16[128,4096]{1,0:T(8,128)(2,1)}, u32[]{:S(2)}) %copy-start.1) | copy-done | bytes 1048600
  3.1 0.0 copy-start.2
  3.1 0.9 copy-done.2
  4.1 0.0 copy-start.3
  4.1 0.8 copy-done.3
  4.9 0.0 copy-start.4
  4.9 0.8 copy-done.4
  5.7 98.9 %block.1 = bf16[128,1024]{1,0:T(8,128)(2,1)S(1)} custom-call(bf16[128,4096]{1,0:T(8,128)(2,1)S(1)} %copy-done.1, bf16[3,512,1024]{2,1,0:T(8,128)(2,1)S(1)} %copy-done, f32[16,1024]{1,0:T(8,128)S(1)} %bitcast.2, f32[16,1024]{1,0:T(8,128)S(1)} %bitcast.3, bf16[1024,128]{1,0:T(8,128)(2,1)S(1)} %copy-done.2), custom_call_target="tpu_custom_call" | custom-call | tf_op jit(solution)/shard_map/block/pallas_call | solution.py:484
  104.7 0.7 copy.7
Async XLA Ops:
  0.0 1.9 %copy-start = (bf16[3,512,1024]{2,1,0:T(8,128)(2,1)S(1)}, bf16[3,512,1024]{2,1,0:T(8,128)(2,1)}, u32[]{:S(2)}) copy-start(bf16[3,512,1024]{2,1,0:T(8,128)(2,1)} %proj_ref.1) | copy-start | bytes 9437188
  1.9 1.2 %copy-start.1 = (bf16[128,4096]{1,0:T(8,128)(2,1)S(1)}, bf16[128,4096]{1,0:T(8,128)(2,1)}, u32[]{:S(2)}) copy-start(bf16[128,4096]{1,0:T(8,128)(2,1)} %tok_ref.1) | copy-start | bytes 3145732
  3.1 0.9 copy-start.2
  4.1 0.8 copy-start.3
  4.9 0.8 copy-start.4

commit v3 on v2

--- a/solution.py
+++ b/solution.py
@@ -224,7 +224,7 @@
     pl.semaphore_signal(barrier, inc=1, device_id=mate, device_id_type=MESH)
     pl.semaphore_wait(barrier, ctx_count)
 
-    z_copy, x_copy, c_copy, w_copy = {}, {}, {}, {}
+    z_copy, w_copy = {}, {}
     for o in range(1, zc):
         zt = (mz + o) % zc
         z_copy[o] = remote(
@@ -232,11 +232,10 @@
             tzs.at[o], tzr.at[o], at_z(zt),
         )
         z_copy[o].start()
-    x_copy[0] = remote(
+    remote(
         tok_ref.at[my_half, cols(mz)], tokb.at[half_block(mz, mx)],
         txs.at[0], txr.at[0], across,
-    )
-    x_copy[0].start()
+    ).start()
 
     def send_weights(i):
         d = order(i)
@@ -247,25 +246,42 @@
         w_copy[i].start()
 
     send_weights(0)
-    for o in range(1, zc):
-        zs = (mz + zc - o) % zc
-        z_copy[o].wait_recv()
+
+    def source(n):
+        return low * n + (1 - low) * (zc - 1 - n)
+
+    def z_forward(n):
+        zs = source(n)
+        o = (mz - zs + zc) % zc
+
+        @pl.when(zs != mz)
+        def _():
+            here = tokb.at[half_block(zs, mx)]
+            pltpu.make_async_copy(here, here, tzr.at[o]).wait()
+            remote(here, here, txs.at[o], txr.at[o], across).start()
+            remote(here, here, tcs.at[o], tcr.at[o], mate).start()
+
+    def x_forward(n):
+        zs = source(n)
+        o = (mz - zs + zc) % zc
+        here = tokb.at[half_block(zs, 1 - mx)]
+        pltpu.make_async_copy(here, here, txr.at[o]).wait()
+        remote(here, here, tcs.at[zc + o], tcr.at[zc + o], mate).start()
+
+    def tokens_here(n):
+        zs = source(n)
+        o = (mz - zs + zc) % zc
         here = tokb.at[half_block(zs, mx)]
-        x_copy[o] = remote(here, here, txs.at[o], txr.at[o], across)
-        x_copy[o].start()
-        c_copy[o] = remote(here, here, tcs.at[o], tcr.at[o], mate)
-        c_copy[o].start()
-    for i in range(1, zc):
-        send_weights(i)
-    for o in range(zc):
-        zs = (mz + zc - o) % zc
-        x_copy[o].wait_recv()
-        here = tokb.at[half_block(zs, 1 - mx)]
-        c_copy[zc + o] = remote(here, here, tcs.at[zc + o], tcr.at[zc + o], mate)
-        c_copy[zc + o].start()
-    for key in c_copy:
-        c_copy[key].wait_recv()
-    own_tok.wait()
+
+        @pl.when(zs != mz)
+        def _():
+            pltpu.make_async_copy(here, here, tcr.at[o]).wait()
+
+        @pl.when(zs == mz)
+        def _():
+            own_tok.wait()
+
+        pltpu.make_async_copy(here, here, tcr.at[zc + o]).wait()
 
     def hop(d, t):
         to = mz + 2 * (d >= held).astype(jnp.int32) - 1
@@ -300,6 +316,30 @@
             sendb[d, k, tile_rows(t), :] = (mine[k] + before[k]).astype(jnp.bfloat16)
         hop(d, t).start()
 
+    def first_products(d, t):
+        mine = products(d, t)
+        for k in range(3):
+            sendb[d, k, tile_rows(t), :] = mine[k].astype(jnp.bfloat16)
+        hop(d, t).start()
+
+    z_forward(0)
+    for n in range(zc):
+        if n + 1 < zc:
+            z_forward(n + 1)
+        x_forward(n)
+        if n + 1 == zc - 1:
+            for i in range(1, zc):
+                send_weights(i)
+        tokens_here(n)
+
+        @pl.when(at_end)
+        def _():
+            if n == 0:
+                weights_here(0)
+            for part in range(PAIR * rows // tile):
+                flow = n * (PAIR * rows // tile) + part
+                first_products(near(0), low * flow + (1 - low) * (tiles - 1 - flow))
+
     @pl.when(interior)
     def _():
         for j in range(held):
@@ -308,13 +348,13 @@
 
             @pl.loop(0, tiles)
             def _(t):
-                pass_on(near(j), t)
+                pass_on(near(j), low * t + (1 - low) * (tiles - 1 - t))
 
                 @pl.when(t > 0)
                 def _():
-                    pass_on(far(j), t - 1)
-
-            pass_on(far(j), tiles - 1)
+                    pass_on(far(j), low * (tiles - t) + (1 - low) * (t - 1))
+
+            pass_on(far(j), (1 - low) * (tiles - 1))
 
     wide = (CHUNKS, width)
     zero = jnp.zeros(wide, jnp.float32)
@@ -404,15 +444,12 @@
 
     @pl.when(at_end)
     def _():
-        for j in range(held):
+        for j in range(1, held):
             weights_here(2 * j)
 
             @pl.loop(0, tiles)
             def _(t):
-                mine = products(near(j), t)
-                for k in range(3):
-                    sendb[near(j), k, tile_rows(t), :] = mine[k].astype(jnp.bfloat16)
-                hop(near(j), t).start()
+                first_products(near(j), low * t + (1 - low) * (tiles - 1 - t))
 
         for j in range(held):
             weights_here(2 * j + 1)
@@ -420,7 +457,8 @@
                 own_par[3 * j + n].wait()
 
             @pl.loop(0, tiles)
-            def _(t):
+            def _(n):
+                t = low * (tiles - 1 - n) + (1 - low) * n
                 mine = products(far(j), t)
                 before = arrived(far(j), t)
                 sums = [mine[k] + before[k] for k in range(3)]
@@ -450,9 +488,15 @@
                 hop(near(j), t).wait_send()
                 hop(far(j), t).wait_send()
 
-    for group_of in (z_copy, x_copy, c_copy, w_copy):
+    for group_of in (z_copy, w_copy):
         for key in group_of:
             group_of[key].wait_send()
+    sent = tokb.at[half_block(mz, mx)]
+    for o in range(zc):
+        remote(sent, sent, txs.at[o], txr.at[o], across).wait_send()
+        remote(sent, sent, tcs.at[zc + o], tcr.at[zc + o], mate).wait_send()
+        if o > 0:
+            remote(sent, sent, tcs.at[o], tcr.at[o], mate).wait_send()
     for d in range(zc):
         owner_row = 0 if d < held else zc - 1
         for x in range(PAIR):
@@ -484,7 +528,7 @@
     return pl.pallas_call(
         block_kernel,
         out_shape=jax.ShapeDtypeStruct((rows, channels), bf16),
-        in_specs=[pl.BlockSpec(memory_space=pl.ANY)] * 5,
+        in_specs=[pl.BlockSpec(memory_space=pltpu.HBM)] * 5,
         out_specs=pl.BlockSpec(memory_space=pltpu.VMEM),
         scratch_shapes=[
             pltpu.VMEM((seq, PAIR * depth), bf16),
@@ -520,7 +564,7 @@
     return (
         ctx_count == CHUNKS and lax.axis_size("ch") % 2 == 0
         and channels == ctx_count * LANES and rows % (16 * PIECES) == 0 and depth % 128 == 0
-        and (rows * ctx_count) % TILE == 0 and tap_count % 8 == 0 and tap_count <= rows
+        and PAIR * rows % TILE == 0 and tap_count % 8 == 0 and tap_count <= rows
         and rows * ctx_count <= 2048
     )
 

time: 106 us -> 108 us (1.019)
  Pallas kernels: 98.9 us -> 101 us
    pallas_call x1, Pallas kernels: 98.9 us -> 101 us  [per_device_kernels(): pl.pallas_call(block_kernel, out_shape=jax.ShapeDtypeStruct((rows, channe...]
where the time goes in v3:
time: 108 us; the launch traced here: 107 us
  Pallas kernels  101 us (94%)
  local copies, waits for them, and re-layouts  6.45 us (6%)
    pallas_call x1, Pallas kernels, per_device_kernels(): pl.pallas_call(block_kernel, out_shape=jax.ShapeDtypeStruct((rows, channe...  101 us
    unnamed x11, local copies, waits for them, and re-layouts  6.45 us

profile of v3, /device:TPU:0, one launch (start us, length us, event | category | flops | bytes accessed | tf_op | source)
XLA Modules:
  0.0 107.5 jit_solution(15057147640310923294)
XLA Ops:
  0.0 0.0 copy-start
  0.0 1.9 %copy-done = bf16[3,512,1024]{2,1,0:T(8,128)(2,1)S(1)} copy-done((bf16[3,512,1024]{2,1,0:T(8,128)(2,1)S(1)}, bf16[3,512,1024]{2,1,0:T(8,128)(2,1)}, u32[]{:S(2)}) %copy-start) | copy-done | bytes 3145752
  1.9 0.0 copy-start.1
  1.9 1.2 %copy-done.1 = bf16[128,4096]{1,0:T(8,128)(2,1)S(1)} copy-done((bf16[128,4096]{1,0:T(8,128)(2,1)S(1)}, bf16[128,4096]{1,0:T(8,128)(2,1)}, u32[]{:S(2)}) %copy-start.1) | copy-done | bytes 1048600
  3.1 0.0 copy-start.2
  3.1 0.9 copy-done.2
  4.1 0.0 copy-start.3
  4.1 0.8 copy-done.3
  4.9 0.0 copy-start.4
  4.9 0.8 copy-done.4
  5.7 101.0 %block.1 = bf16[128,1024]{1,0:T(8,128)(2,1)S(1)} custom-call(bf16[128,4096]{1,0:T(8,128)(2,1)S(1)} %copy-done.1, bf16[3,512,1024]{2,1,0:T(8,128)(2,1)S(1)} %copy-done, f32[16,1024]{1,0:T(8,128)S(1)} %bitcast.2, f32[16,1024]{1,0:T(8,128)S(1)} %bitcast.3, bf16[1024,128]{1,0:T(8,128)(2,1)S(1)} %copy-done.2), custom_call_target="tpu_custom_call" | custom-call | tf_op jit(solution)/shard_map/block/pallas_call | solution.py:528
  106.8 0.7 copy.7
Async XLA Ops:
  0.0 1.9 %copy-start = (bf16[3,512,1024]{2,1,0:T(8,128)(2,1)S(1)}, bf16[3,512,1024]{2,1,0:T(8,128)(2,1)}, u32[]{:S(2)}) copy-start(bf16[3,512,1024]{2,1,0:T(8,128)(2,1)} %proj_ref.1) | copy-start | bytes 9437188
  1.9 1.2 %copy-start.1 = (bf16[128,4096]{1,0:T(8,128)(2,1)S(1)}, bf16[128,4096]{1,0:T(8,128)(2,1)}, u32[]{:S(2)}) copy-start(bf16[128,4096]{1,0:T(8,128)(2,1)} %tok_ref.1) | copy-start | bytes 3145732
  3.1 0.9 copy-start.2
  4.1 0.8 copy-start.3
  4.9 0.8 copy-start.4
